TPU v7x, 256 devices: a whole 4x4x8 slice. The times are simulated.
256 devices in a mesh: fluid: 64 (over x, z, core), metal: 4 (over y).
Axes of the slice: x: 4, y: 4, z: 8, core: 2. Of those that a mesh axis runs over, the one named last changes fastest.
Arguments:
- fluid_x: bfloat16 [16384, 512], P('fluid', 'metal'), may hold values from -32 to 32
- metal_x: bfloat16 [8192, 512], P('fluid', 'metal'), may hold values from -32 to 32
- w_rf: bfloat16 [512, 512], P(None, 'metal'), may hold values from -0.5 to 0.5
- w_vf: bfloat16 [512, 512], P(None, 'metal'), may hold values from -0.25 to 0.25
- w_rm: bfloat16 [512, 512], P(None, 'metal'), may hold values from -0.5 to 0.5
- w_vm: bfloat16 [512, 512], P(None, 'metal'), may hold values from -0.25 to 0.25
- fluid_grad: bfloat16 [16384, 512], P('fluid', 'metal'), may hold values from -6 to 6
- metal_grad: bfloat16 [8192, 512], P('fluid', 'metal'), may hold values from -6 to 6
- pair_list: int32 [2048, 2], P('fluid'), may hold values from 0 to 63, as said below
- pair_count: int32 [64], P('fluid'), may hold values from 2 to 32, as said below
Outputs:
- fluid_out: bfloat16 [16384, 512], P('fluid', 'metal')
- metal_out: bfloat16 [8192, 512], P('fluid', 'metal')
- fluid_dx: bfloat16 [16384, 512], P('fluid', 'metal')
- metal_dx: bfloat16 [8192, 512], P('fluid', 'metal')
- weight_grads: float32 [4, 512, 512], P(None, None, 'metal')
Inputs may be any that keep to these rules, and one draw needn't show every extreme that they name: `pair_list`: column 0 is a local fluid block below 2, column 1 a metal block below 64. The first pair_count[d] entries of fluid index d are distinct pairs; every fluid block of every index and every metal block stands in some live entry; entries past the count hold valid indices and are ignored. `pair_count`: some fluid index has all 32 slots live.
All inputs are finite; a program needn't handle non-finite values.
Results may differ from a plain program's by a relative error of at most 0.0179.
The roundings to bfloat16 on the way count: a program that leaves them out, or rounds other values in their place, can miss the bound.
Values may be sent and summed in bfloat16 or wider, within the bound.
No kernel may reach another device: no remote copies, remote signals or barrier semaphores. Data moves between devices by JAX's collectives and lax.ppermute only.
A program may use at most 128 MiB of HBM per device.

v0:
```python
import math
import jax
import jax.numpy as jnp
from jax import lax
from jax.sharding import PartitionSpec as P

D = 512
H = 8
BLK = 128
LOWEST = -1e30


def project(inputs, weight):
    return jnp.dot(inputs, weight, preferred_element_type=jnp.float32).astype(jnp.bfloat16)


def back_project(grads, weight):
    return lax.dot_general(
        grads, weight, (((1,), (1,)), ((), ())), preferred_element_type=jnp.float32
    )


def outer_rows(inputs, grads):
    return lax.dot_general(
        inputs, grads, (((0,), (0,)), ((), ())), preferred_element_type=jnp.float32
    )


def body(fluid_x, metal_x, w_rf, w_vf, w_rm, w_vm, fluid_grad, metal_grad, pair_list, pair_count):
    head_size = D // H
    local_heads = w_rf.shape[1] // head_size
    feature_cols = w_rf.shape[1]
    fluid_rows = fluid_x.shape[0]
    blocks = fluid_rows // BLK
    metal_blocks = lax.axis_size("fluid")
    metal_rows = metal_blocks * BLK
    slot_total = pair_list.shape[0]
    batch_size = math.gcd(slot_total, 16)
    inv_root = 1.0 / math.sqrt(head_size)
    live_count = pair_count[0]
    loop_turns = slot_total // batch_size
    fluid_full, metal_full = (
        lax.all_gather(fluid_x, "metal", axis=1, tiled=True),
        lax.all_gather(metal_x, "metal", axis=1, tiled=True),
    )
    fluid_keys = project(fluid_full, w_rf)
    fluid_values = project(fluid_full, w_vf)
    metal_keys = project(metal_full, w_rm)
    metal_values = project(metal_full, w_vm)
    keys_all, values_all = (
        lax.all_gather(metal_keys, "fluid", axis=0, tiled=True),
        lax.all_gather(metal_values, "fluid", axis=0, tiled=True),
    )
    fkey_tiles = fluid_keys.reshape(blocks, BLK, local_heads, head_size)
    fval_tiles = fluid_values.reshape(blocks, BLK, local_heads, head_size)
    mkey_tiles = keys_all.reshape(metal_blocks, BLK, local_heads, head_size)
    mval_tiles = values_all.reshape(metal_blocks, BLK, local_heads, head_size)

    def batch_pairs(number):
        entries = lax.dynamic_slice_in_dim(pair_list, number * batch_size, batch_size, 0)
        slot_index = number * batch_size + jnp.arange(batch_size, dtype=jnp.int32)
        frows = entries[:, 0]
        mrows = entries[:, 1]
        scores = (
            jnp.einsum(
                "pahd,pbhd->phab",
                fkey_tiles[frows],
                mkey_tiles[mrows],
                preferred_element_type=jnp.float32,
            )
            * inv_root
        )
        return (frows, mrows, slot_index < live_count, scores)

    def max_pass(number, state):
        row_max, col_max = state
        frows, mrows, active, scores = batch_pairs(number)
        live = active[:, None, None]
        row_max = row_max.at[frows].max(jnp.where(live, jnp.max(scores, axis=3), LOWEST))
        col_max = col_max.at[mrows].max(jnp.where(live, jnp.max(scores, axis=2), LOWEST))
        return (row_max, col_max)

    row_max, col_local = lax.fori_loop(
        0,
        loop_turns,
        max_pass,
        (
            jnp.full((blocks, local_heads, BLK), LOWEST, jnp.float32),
            jnp.full((metal_blocks, local_heads, BLK), LOWEST, jnp.float32),
        ),
    )
    col_max = lax.pmax(col_local, "fluid")

    def sum_pass(number, state):
        row_sum, fluid_num, col_sum, metal_num = state
        frows, mrows, active, scores = batch_pairs(number)
        live = active[:, None, None, None]
        row_exp = jnp.where(live, jnp.exp(scores - row_max[frows][:, :, :, None]), 0.0)
        col_exp = jnp.where(live, jnp.exp(scores - col_max[mrows][:, :, None, :]), 0.0)
        row_sum = row_sum.at[frows].add(jnp.sum(row_exp, axis=3))
        col_sum = col_sum.at[mrows].add(jnp.sum(col_exp, axis=2))
        fluid_num = fluid_num.at[frows].add(
            jnp.einsum(
                "phab,pbhd->pahd",
                row_exp.astype(jnp.bfloat16),
                mval_tiles[mrows],
                preferred_element_type=jnp.float32,
            )
        )
        metal_num = metal_num.at[mrows].add(
            jnp.einsum(
                "phab,pahd->pbhd",
                col_exp.astype(jnp.bfloat16),
                fval_tiles[frows],
                preferred_element_type=jnp.float32,
            )
        )
        return (row_sum, fluid_num, col_sum, metal_num)

    row_sum, fluid_num, col_sum, metal_num = lax.fori_loop(
        0,
        loop_turns,
        sum_pass,
        (
            jnp.zeros((blocks, local_heads, BLK), jnp.float32),
            jnp.zeros((blocks, BLK, local_heads, head_size), jnp.float32),
            jnp.zeros((metal_blocks, local_heads, BLK), jnp.float32),
            jnp.zeros((metal_blocks, BLK, local_heads, head_size), jnp.float32),
        ),
    )
    fluid_out = (
        (fluid_num / row_sum.transpose(0, 2, 1)[:, :, :, None])
        .reshape(fluid_rows, feature_cols)
        .astype(jnp.bfloat16)
    )
    num_rows = metal_num.reshape(metal_rows, feature_cols)
    total_rows = col_sum.transpose(0, 2, 1).reshape(metal_rows, local_heads)
    own_num, own_sum = (
        lax.psum_scatter(num_rows, "fluid", scatter_dimension=0, tiled=True),
        lax.psum_scatter(total_rows, "fluid", scatter_dimension=0, tiled=True),
    )
    metal_out = (
        (own_num.reshape(BLK, local_heads, head_size) / own_sum[:, :, None])
        .reshape(BLK, feature_cols)
        .astype(jnp.bfloat16)
    )
    scaled_grad = (
        (metal_grad.astype(jnp.float32).reshape(BLK, local_heads, head_size) / own_sum[:, :, None])
        .reshape(BLK, feature_cols)
        .astype(jnp.bfloat16)
    )
    scaled_all, output_all = (
        lax.all_gather(scaled_grad, "fluid", axis=0, tiled=True),
        lax.all_gather(metal_out, "fluid", axis=0, tiled=True),
    )
    delta_f = jnp.sum(
        (fluid_grad.astype(jnp.float32) * fluid_out.astype(jnp.float32)).reshape(
            fluid_rows, local_heads, head_size
        ),
        axis=2,
    )
    delta_m = jnp.sum(
        (scaled_all.astype(jnp.float32) * output_all.astype(jnp.float32)).reshape(
            metal_blocks, BLK, local_heads, head_size
        ),
        axis=3,
    )
    grad_tiles = fluid_grad.reshape(blocks, BLK, local_heads, head_size)
    scaled_tiles = scaled_all.reshape(metal_blocks, BLK, local_heads, head_size)
    dfluid_tiles = delta_f.reshape(blocks, BLK, local_heads)

    def grad_pass(number, state):
        grad_rf, grad_vf, grad_rm, grad_vm = state
        frows, mrows, active, scores = batch_pairs(number)
        live = active[:, None, None, None]
        attn = jnp.where(
            live,
            jnp.exp(scores - row_max[frows][:, :, :, None]) / row_sum[frows][:, :, :, None],
            0.0,
        )
        col_exp = jnp.where(live, jnp.exp(scores - col_max[mrows][:, :, None, :]), 0.0)
        fluid_term = jnp.einsum(
            "pahd,pbhd->phab",
            grad_tiles[frows],
            mval_tiles[mrows],
            preferred_element_type=jnp.float32,
        )
        metal_term = jnp.einsum(
            "pahd,pbhd->phab",
            fval_tiles[frows],
            scaled_tiles[mrows],
            preferred_element_type=jnp.float32,
        )
        dscore = attn * (fluid_term - dfluid_tiles[frows].transpose(0, 2, 1)[:, :, :, None])
        dscore = dscore + col_exp * (metal_term - delta_m[mrows].transpose(0, 2, 1)[:, :, None, :])
        dscore_weight = dscore.astype(jnp.bfloat16)
        grad_rf = grad_rf.at[frows].add(
            jnp.einsum(
                "phab,pbhd->pahd",
                dscore_weight,
                mkey_tiles[mrows],
                preferred_element_type=jnp.float32,
            )
            * inv_root
        )
        grad_vf = grad_vf.at[frows].add(
            jnp.einsum(
                "phab,pbhd->pahd",
                col_exp.astype(jnp.bfloat16),
                scaled_tiles[mrows],
                preferred_element_type=jnp.float32,
            )
        )
        grad_rm = grad_rm.at[mrows].add(
            jnp.einsum(
                "phab,pahd->pbhd",
                dscore_weight,
                fkey_tiles[frows],
                preferred_element_type=jnp.float32,
            )
            * inv_root
        )
        grad_vm = grad_vm.at[mrows].add(
            jnp.einsum(
                "phab,pahd->pbhd",
                attn.astype(jnp.bfloat16),
                grad_tiles[frows],
                preferred_element_type=jnp.float32,
            )
        )
        return (grad_rf, grad_vf, grad_rm, grad_vm)

    grad_rf, grad_vf, grad_rm, grad_vm = lax.fori_loop(
        0,
        loop_turns,
        grad_pass,
        (
            jnp.zeros((blocks, BLK, local_heads, head_size), jnp.float32),
            jnp.zeros((blocks, BLK, local_heads, head_size), jnp.float32),
            jnp.zeros((metal_blocks, BLK, local_heads, head_size), jnp.float32),
            jnp.zeros((metal_blocks, BLK, local_heads, head_size), jnp.float32),
        ),
    )
    rf_rounded = grad_rf.reshape(fluid_rows, feature_cols).astype(jnp.bfloat16)
    vf_rounded = grad_vf.reshape(fluid_rows, feature_cols).astype(jnp.bfloat16)
    fluid_part = back_project(rf_rounded, w_rf) + back_project(vf_rounded, w_vf)
    fluid_part, weight_rf, weight_vf = (
        fluid_part,
        outer_rows(fluid_full, rf_rounded),
        outer_rows(fluid_full, vf_rounded),
    )
    rm_rounded = lax.psum_scatter(
        grad_rm.reshape(metal_rows, feature_cols), "fluid", scatter_dimension=0, tiled=True
    ).astype(jnp.bfloat16)
    vm_rounded = lax.psum_scatter(
        grad_vm.reshape(metal_rows, feature_cols), "fluid", scatter_dimension=0, tiled=True
    ).astype(jnp.bfloat16)
    metal_part = back_project(rm_rounded, w_rm) + back_project(vm_rounded, w_vm)
    weight_rm = outer_rows(metal_full, rm_rounded)
    weight_vm = outer_rows(metal_full, vm_rounded)
    fluid_dx, metal_dx = (
        lax.psum_scatter(fluid_part, "metal", scatter_dimension=1, tiled=True),
        lax.psum_scatter(metal_part, "metal", scatter_dimension=1, tiled=True),
    )
    weight_grads = lax.psum(jnp.stack([weight_rf, weight_vf, weight_rm, weight_vm]), "fluid")
    return (
        fluid_out,
        metal_out,
        fluid_dx.astype(jnp.bfloat16),
        metal_dx.astype(jnp.bfloat16),
        weight_grads,
    )


def solution(mesh):
    placed = (
        P("fluid", "metal"),
        P("fluid", "metal"),
        P(None, "metal"),
        P(None, "metal"),
        P(None, "metal"),
        P(None, "metal"),
        P("fluid", "metal"),
        P("fluid", "metal"),
        P("fluid", None),
        P("fluid"),
    )
    return jax.shard_map(
        body,
        mesh=mesh,
        in_specs=placed,
        out_specs=(
            P("fluid", "metal"),
            P("fluid", "metal"),
            P("fluid", "metal"),
            P("fluid", "metal"),
            P(None, None, "metal"),
        ),
        check_vma=False,
    )
```

profile of v0, /device:TPU:2, one launch (start us, length us, event | category | flops | bytes accessed | tf_op | source)
XLA Modules:
  0.0 1555.2 jit_solution(13822160661187020611)
XLA Ops:
  7.2 11.8 all_gather.19
  22.6 11.7 all_gather.18
  34.7 64.7 %all-gather.5.cloned.1.call-done = bf16[8192,128]{1,0:T(8,128)(2,1)} async-done(((bf16[128,128]{1,0:T(8,128)(2,1)}), bf16[8192,128]{1,0:T(8,128)(2,1)}) %all-gather.5.cloned.1.call-update) | async-done | bytes 2097168 | tf_op jit(solution)/shard_map/all_gather | solution.py:51
  99.4 8.2 reshape.334
  107.6 23.2 %while.53 = (s32[]{:T(128)}, f32[2,2,128]{2,1,0:T(2,128)S(1)}, f32[64,2,128]{2,1,0:T(2,128)S(1)}, s32[32,2]{0,1:T(2,128)S(1)}, s32[]{:T(128)}, /*index=5*/bf16[2...) while((s32[]{:T(128)}, f32[2,2,128]{2,1,0:T(2,128)S(1)}, ...), condition=%wide.region_5.6_spmd, body=%wide.region_0.5_spmd.sunk | while | flops 68692104 | bytes 3351623 | solution.py:83
  131.9 45.8 %all-gather.7.cloned.1.call-done = bf16[8192,128]{1,0:T(8,128)(2,1)} async-done(((bf16[128,128]{1,0:T(8,128)(2,1)}), bf16[8192,128]{1,0:T(8,128)(2,1)}) %all-gather.7.cloned.1.call-update) | async-done | bytes 2097168 | tf_op jit(solution)/shard_map/all_gather | solution.py:52
  177.7 8.3 reshape.335
  185.9 161.9 %all-reduce.3.cloned.1.call-done = f32[64,2,128]{2,1,0:T(2,128)} async-done(((f32[64,2,128]{2,1,0:T(2,128)}), f32[64,2,128]{2,1,0:T(2,128)}) %all-reduce.3.cloned.1.call-update) | async-done | bytes 65552 | tf_op jit(solution)/shard_map/pmax | solution.py:92
  350.3 67.5 %while.54 = (s32[]{:T(128)}, f32[2,2,128]{2,1,0:T(2,128)S(1)}, f32[2,128,2,64]{1,3,2,0:T(8,128)S(1)}, f32[64,2,128]{2,1,0:T(2,128)S(1)}, f32[64,128,2,64]{1,3,2,...) while((s32[]{:T(128)}, f32[2,2,128]{2,1,0:T(2,128)S(1)}, ...), condition=%wide.region_14.15_spmd, body=%wide.region_7.14_spmd.sunk | while | flops 209717376 | bytes 25437748 | solution.py:120
  358.2 5.7 gather_fusion.4
  391.6 5.7 gather_fusion.4
  431.3 130.0 %reduce-scatter.19.cloned.1.call-done = f32[128,2]{1,0:T(8,128)} async-done(((f32[8192,2]{1,0:T(8,128)}), f32[128,2]{1,0:T(8,128)}) %reduce-scatter.19.cloned.1.call-update) | async-done | bytes 1040
  562.2 145.2 %reduce-scatter.9.cloned.1.call-done = f32[128,128]{0,1:T(8,128)} async-done(((f32[8192,128]{0,1:T(8,128)}), f32[128,128]{0,1:T(8,128)}) %reduce-scatter.9.cloned.1.call-update) | async-done | bytes 65552 | tf_op jit(solution)/shard_map/reduce_scatter | solution.py:139
  710.1 72.3 %all-gather.9.cloned.1.call-done = bf16[8192,128]{0,1:T(8,128)(2,1)} async-done(((bf16[128,128]{0,1:T(8,128)(2,1)}), bf16[8192,128]{0,1:T(8,128)(2,1)}) %all-gather.9.cloned.1.call-update) | async-done | bytes 2097168 | tf_op jit(solution)/shard_map/all_gather | solution.py:153
  782.4 74.9 %all-gather.11.cloned.1.call-done = bf16[8192,128]{0,1:T(8,128)(2,1)} async-done(((bf16[128,128]{0,1:T(8,128)(2,1)}), bf16[8192,128]{0,1:T(8,128)(2,1)}) %all-gather.11.cloned.1.call-update) | async-done | bytes 2097168 | tf_op jit(solution)/shard_map/all_gather | solution.py:154
  877.5 131.7 %while.55 = (s32[]{:T(128)}, f32[2,128,2,64]{1,3,2,0:T(8,128)S(1)}, f32[2,128,2,64]{1,3,2,0:T(8,128)S(1)}, f32[64,128,2,64]{1,3,2,0:T(8,128)}, f32[64,128,2,64]{...) while((s32[]{:T(128)}, f32[2,128,2,64]{1,3,2,0:T(8,128)S(1)}, ...), condition=%wide.region_24.25_spmd, body=%wide.region_19.24_spmd.sunk | while | flops 482347136 | bytes 61189336 | solution.py:233
  895.4 5.7 gather_fusion.8
  961.1 5.7 gather_fusion.8
  1023.8 5.3 copy.185
  1031.5 129.8 %reduce-scatter.15.cloned.1.call-done = f32[128,128]{0,1:T(8,128)} async-done(((f32[8192,128]{0,1:T(8,128)}), f32[128,128]{0,1:T(8,128)}) %reduce-scatter.15.cloned.1.call-update) | async-done | bytes 65552 | tf_op jit(solution)/shard_map/reduce_scatter | solution.py:255
  1162.3 145.3 %reduce-scatter.13.cloned.1.call-done = f32[128,128]{0,1:T(8,128)} async-done(((f32[8192,128]{0,1:T(8,128)}), f32[128,128]{0,1:T(8,128)}) %reduce-scatter.13.cloned.1.call-update) | async-done | bytes 65552 | tf_op jit(solution)/shard_map/reduce_scatter | solution.py:252
  1312.6 20.7 %reduce-scatter.11.cloned.1.call-done = f32[256,128]{1,0:T(8,128)} async-done(((f32[256,512]{1,0:T(8,128)}), f32[256,128]{1,0:T(8,128)}) %reduce-scatter.11.cloned.1.call-update) | async-done | bytes 131088 | tf_op jit(solution)/shard_map/reduce_scatter | solution.py:262
  1334.8 188.6 %all-reduce.5.cloned.1.call-done = f32[4,512,128]{1,2,0:T(8,128)} async-done(((f32[4,512,128]{1,2,0:T(8,128)}), f32[4,512,128]{1,2,0:T(8,128)}) %all-reduce.5.cloned.1.call-update) | async-done | bytes 1048592 | tf_op jit(solution)/shard_map/psum | solution.py:265
  1525.9 20.6 %reduce-scatter.17.cloned.1.call-done = f32[128,128]{1,0:T(8,128)} async-done(((f32[128,512]{1,0:T(8,128)}), f32[128,128]{1,0:T(8,128)}) %reduce-scatter.17.cloned.1.call-update) | async-done | bytes 65552 | tf_op jit(solution)/shard_map/reduce_scatter | solution.py:263
  (269 shorter events, 270.7 us)
Async XLA Ops:
  7.2 27.2 %copy-start = (bf16[512,128]{1,0:T(8,128)(2,1)S(1)}, bf16[512,128]{1,0:T(8,128)(2,1)}, u32[]{:S(2)}) copy-start(bf16[512,128]{1,0:T(8,128)(2,1)} %param.18) | copy-start | bytes 393220
  7.2 92.2 %all-gather.5.cloned.1.call-start = ((), (), s32[]{:S(2)}) async-start(), calls=%async_computation.6 | async-start | bytes 2129920 | tf_op jit(solution)/shard_map/all_gather | solution.py:51
  19.0 15.3 copy-start.8
  20.8 156.9 %all-gather.7.cloned.1.call-start = ((), (), s32[]{:S(2)}) async-start(), calls=%async_computation.7 | async-start | bytes 2129920 | tf_op jit(solution)/shard_map/all_gather | solution.py:52
  22.6 325.3 %all-reduce.3.cloned.1.call-start = ((), (), s32[]{:S(2)}) async-start(), calls=%async_computation.8 | async-start | bytes 131072 | tf_op jit(solution)/shard_map/pmax | solution.py:92
  34.3 97.2 %copy-start.6 = (bf16[256,512]{1,0:T(8,128)(2,1)}, bf16[256,512]{1,0:T(8,128)(2,1)S(1)}, u32[]{:S(2)}) copy-start(bf16[256,512]{1,0:T(8,128)(2,1)S(1)} %all_gather.18) | copy-start | bytes 786436
  34.7 72.9 %copy-start.22 = (s32[32,2]{0,1:T(2,128)S(1)}, s32[32,2]{0,1:T(2,128)}, u32[]{:S(2)}) copy-start(s32[32,2]{0,1:T(2,128)} %param.24) | copy-start | bytes 772
  107.6 24.0 %copy-start.13 = (bf16[512,128]{1,0:T(8,128)(2,1)S(1)}, bf16[512,128]{1,0:T(8,128)(2,1)}, u32[]{:S(2)}) copy-start(bf16[512,128]{1,0:T(8,128)(2,1)} %param.19) | copy-start | bytes 393220
  131.5 429.8 %reduce-scatter.19.cloned.1.call-start = ((), (), s32[]{:S(2)}) async-start(), calls=%async_computation.17 | async-start | bytes 4259840
  410.1 3.9 copy-start.1
  420.5 286.9 %reduce-scatter.9.cloned.1.call-start = ((), (), s32[]{:S(2)}) async-start(), calls=%async_computation.9 | async-start | bytes 4259840 | tf_op jit(solution)/shard_map/reduce_scatter | solution.py:139
  430.4 279.3 %copy-start.20 = (bf16[256,128]{1,0:T(8,128)(2,1)S(1)}, bf16[256,128]{1,0:T(8,128)(2,1)}, u32[]{:S(2)}) copy-start(bf16[256,128]{1,0:T(8,128)(2,1)} %param.22) | copy-start | bytes 196612
  430.5 351.9 %all-gather.9.cloned.1.call-start = ((), (), s32[]{:S(2)}) async-start(), calls=%async_computation.10 | async-start | bytes 2129920 | tf_op jit(solution)/shard_map/all_gather | solution.py:153
  708.9 148.3 %all-gather.11.cloned.1.call-start = ((), (), s32[]{:S(2)}) async-start(), calls=%async_computation.11 | async-start | bytes 2129920 | tf_op jit(solution)/shard_map/all_gather | solution.py:154
  709.7 451.6 %reduce-scatter.15.cloned.1.call-start = ((), (), s32[]{:S(2)}) async-start(), calls=%async_computation.14 | async-start | bytes 4259840 | tf_op jit(solution)/shard_map/reduce_scatter | solution.py:255
  710.0 149.9 %copy-start.11 = (bf16[2,128,2,64]{1,0,3,2:T(2,128)(2,1)}, bf16[2,128,2,64]{1,0,3,2:T(2,128)(2,1)S(1)}, u32[]{:S(2)}) copy-start(bf16[2,128,2,64]{1,0,3,2:T(2,128)(2,1)S(1)} %copy.104) | copy-start | bytes 196612
  1019.1 288.5 %reduce-scatter.13.cloned.1.call-start = ((), (), s32[]{:S(2)}) async-start(), calls=%async_computation.13 | async-start | bytes 4259840 | tf_op jit(solution)/shard_map/reduce_scatter | solution.py:252
  1029.1 304.2 %reduce-scatter.11.cloned.1.call-start = ((), (), s32[]{:S(2)}) async-start(), calls=%async_computation.12 | async-start | bytes 655360 | tf_op jit(solution)/shard_map/reduce_scatter | solution.py:262
  1029.1 132.1 %copy-start.9 = (bf16[128,512]{1,0:T(8,128)(2,1)S(1)}, bf16[128,512]{1,0:T(8,128)(2,1)}, u32[]{:S(2)}) copy-start(bf16[128,512]{1,0:T(8,128)(2,1)} %copy-done.8) | copy-start | bytes 393220
  1031.0 492.3 %all-reduce.5.cloned.1.call-start = ((), (), s32[]{:S(2)}) async-start(), calls=%async_computation.16 | async-start | bytes 2097152 | tf_op jit(solution)/shard_map/psum | solution.py:265
  1031.5 278.4 %copy-start.15 = (bf16[512,128]{1,0:T(8,128)(2,1)S(1)}, bf16[512,128]{1,0:T(8,128)(2,1)}, u32[]{:S(2)}) copy-start(bf16[512,128]{1,0:T(8,128)(2,1)} %param.20) | copy-start | bytes 393220
  1162.3 147.8 %copy-start.16 = (bf16[512,128]{1,0:T(8,128)(2,1)S(1)}, bf16[512,128]{1,0:T(8,128)(2,1)}, u32[]{:S(2)}) copy-start(bf16[512,128]{1,0:T(8,128)(2,1)} %param.21) | copy-start | bytes 393220
  1162.3 147.8 %copy-start.21 = (f32[128,128]{0,1:T(8,128)S(1)}, f32[128,128]{0,1:T(8,128)}, u32[]{:S(2)}) copy-start(f32[128,128]{0,1:T(8,128)} %reduce-scatter.15.cloned.1.call-done) | copy-start | bytes 196612
  1309.8 236.7 %reduce-scatter.17.cloned.1.call-start = ((), (), s32[]{:S(2)}) async-start(), calls=%async_computation.15 | async-start | bytes 327680 | tf_op jit(solution)/shard_map/reduce_scatter | solution.py:263
  (28 other events, 49.7 us)
Sparse Core Ops, SparseCore 0:
  20.9 78.4 all-gather.4
  102.7 74.9 all-gather.6
  181.8 166.0 all-reduce.2
  420.7 140.5 reduce-scatter.18
  565.3 142.0 reduce-scatter.8
  710.7 71.6 all-gather.8
  785.8 71.3 all-gather.10
  1019.2 141.9 reduce-scatter.14
  1165.4 142.1 reduce-scatter.12
  1310.2 23.0 reduce-scatter.10
  1337.7 185.6 all-reduce.4
  1525.7 20.7 reduce-scatter.16
where the time goes:
time: 1570 us; the launch traced here: 1560 us
  waiting for transfers between devices  1200 us (76%)
  local copies, waits for them, and re-layouts  209 us (13%)
  other arithmetic  58.9 us (4%)
  matrix products  46.7 us (3%)
  blocking collectives  23.5 us (1%)
    psum x1, waiting for transfers between devices, body(): lax.psum(jnp.stack([weight_rf, weight_vf, weight_rm, weight_vm]), 'fluid')  189 us
    pmax x1, waiting for transfers between devices, body(): col_max = lax.pmax(col_local, 'fluid')  162 us
    reduce_scatter x1, waiting for transfers between devices, body(): lax.psum_scatter(grad_rm.reshape(metal_rows, feature_cols), 'fluid', scat...  145 us
    reduce_scatter x1, waiting for transfers between devices, body(): lax.psum_scatter(num_rows, 'fluid', scatter_dimension=0, tiled=True)  145 us
    unnamed x13, waiting for transfers between devices  131 us
    reduce_scatter x1, waiting for transfers between devices, body(): lax.psum_scatter(grad_vm.reshape(metal_rows, feature_cols), 'fluid', scat...  130 us
    all_gather x1, waiting for transfers between devices, body(): lax.all_gather(metal_out, 'fluid', axis=0, tiled=True)  74.9 us
    all_gather x1, waiting for transfers between devices, body(): lax.all_gather(scaled_grad, 'fluid', axis=0, tiled=True)  72.3 us
  transfers between devices with their start and end apart: 12, of which 12 were waited for; matrix products, arithmetic and copies ran while one was open for 5% of the time, Pallas kernels for 0%

commit v1 on v0

--- a/solution.py
+++ b/solution.py
@@ -48,7 +48,9 @@
     metal_keys = project(metal_full, w_rm)
     metal_values = project(metal_full, w_vm)
     keys_all, values_all = (
-        lax.all_gather(metal_keys, "fluid", axis=0, tiled=True),
+        jnp.concatenate(
+            lax.all_to_all(jnp.stack([metal_keys] * lax.axis_size("fluid")), "fluid", 0, 0), axis=0
+        ),
         lax.all_gather(metal_values, "fluid", axis=0, tiled=True),
     )
     fkey_tiles = fluid_keys.reshape(blocks, BLK, local_heads, head_size)

time: 1570 us -> 1510 us (0.962)
  waiting for transfers between devices: 1200 us -> 1130 us
    all_gather x1 -> x0, waiting for transfers between devices: 64.7 us -> none  [body(): lax.all_gather(metal_keys, 'fluid', axis=0, tiled=True)]
    all_gather x1, waiting for transfers between devices: 45.8 us -> 1.53 us  [body(): lax.all_gather(metal_values, 'fluid', axis=0, tiled=True)]
    all_to_all x0 -> x1, waiting for transfers between devices: none -> 38.2 us  [body(): lax.all_to_all(jnp.stack([metal_keys] * lax.axis_size('fluid')), 'fluid',...]
    unnamed x13 -> x12, waiting for transfers between devices: 131 us -> 131 us
where the time goes in v1:
time: 1510 us; the launch traced here: 1490 us
  waiting for transfers between devices  1130 us (75%)
  local copies, waits for them, and re-layouts  210 us (14%)
  other arithmetic  59 us (4%)
  matrix products  45.2 us (3%)
  blocking collectives  23.2 us (2%)
    psum x1, waiting for transfers between devices, body(): lax.psum(jnp.stack([weight_rf, weight_vf, weight_rm, weight_vm]), 'fluid')  188 us
    pmax x1, waiting for transfers between devices, body(): col_max = lax.pmax(col_local, 'fluid')  162 us
    reduce_scatter x1, waiting for transfers between devices, body(): lax.psum_scatter(grad_rm.reshape(metal_rows, feature_cols), 'fluid', scat...  145 us
    reduce_scatter x1, waiting for transfers between devices, body(): lax.psum_scatter(num_rows, 'fluid', scatter_dimension=0, tiled=True)  145 us
    unnamed x12, waiting for transfers between devices  131 us
    reduce_scatter x1, waiting for transfers between devices, body(): lax.psum_scatter(grad_vm.reshape(metal_rows, feature_cols), 'fluid', scat...  130 us
    all_gather x1, waiting for transfers between devices, body(): lax.all_gather(metal_out, 'fluid', axis=0, tiled=True)  74.7 us
    all_gather x1, waiting for transfers between devices, body(): lax.all_gather(scaled_grad, 'fluid', axis=0, tiled=True)  72.3 us
  transfers between devices with their start and end apart: 12, of which 12 were waited for; matrix products, arithmetic and copies ran while one was open for 5% of the time, Pallas kernels for 0%

profile of v1, /device:TPU:2, one launch (start us, length us, event | category | flops | bytes accessed | tf_op | source)
XLA Modules:
  0.0 1494.8 jit_solution(10302843328401554937)
XLA Ops:
  7.2 11.9 all_gather.16
  22.2 12.2 all-to-all-start
  35.3 11.3 all_gather.15
  46.9 38.2 %all-to-all-done = bf16[64,128,128]{1,2,0:T(8,128)(2,1)S(1)} async-done(((bf16[64,128,128]{1,2,0:T(8,128)(2,1)}), bf16[64,128,128]{1,2,0:T(8,128)(2,1)S(1)}, u32[]{:S(2)}, u32[]{:S(2)}) %all-to-all-start) | async-done | bytes 2097184 | tf_op jit(solution)/shard_map/all_to_all | solution.py:52
  85.2 7.4 copy.101
  92.6 23.3 %while.53 = (s32[]{:T(128)}, f32[2,2,128]{2,1,0:T(2,128)S(1)}, f32[64,2,128]{2,1,0:T(2,128)S(1)}, s32[32,2]{0,1:T(2,128)S(1)}, s32[]{:T(128)}, /*index=5*/bf16[2...) while((s32[]{:T(128)}, f32[2,2,128]{2,1,0:T(2,128)S(1)}, ...), condition=%wide.region_5.6_spmd, body=%wide.region_0.5_spmd.sunk | while | flops 68692104 | bytes 3351623 | solution.py:85
  118.5 8.3 reshape.332
  126.7 161.8 %all-reduce.3.cloned.1.call-done = f32[64,2,128]{2,1,0:T(2,128)} async-done(((f32[64,2,128]{2,1,0:T(2,128)}), f32[64,2,128]{2,1,0:T(2,128)}) %all-reduce.3.cloned.1.call-update) | async-done | bytes 65552 | tf_op jit(solution)/shard_map/pmax | solution.py:94
  291.0 67.5 %while.54 = (s32[]{:T(128)}, f32[2,2,128]{2,1,0:T(2,128)S(1)}, f32[2,128,2,64]{1,3,2,0:T(8,128)S(1)}, f32[64,2,128]{2,1,0:T(2,128)S(1)}, f32[64,128,2,64]{1,3,2,...) while((s32[]{:T(128)}, f32[2,2,128]{2,1,0:T(2,128)S(1)}, ...), condition=%wide.region_14.15_spmd, body=%wide.region_7.14_spmd.sunk | while | flops 209717376 | bytes 25437748 | solution.py:122
  298.8 5.7 gather_fusion.4
  332.3 5.7 gather_fusion.4
  372.0 130.1 %reduce-scatter.19.cloned.1.call-done = f32[128,2]{1,0:T(8,128)} async-done(((f32[8192,2]{1,0:T(8,128)}), f32[128,2]{1,0:T(8,128)}) %reduce-scatter.19.cloned.1.call-update) | async-done | bytes 1040
  502.9 145.3 %reduce-scatter.9.cloned.1.call-done = f32[128,128]{0,1:T(8,128)} async-done(((f32[8192,128]{0,1:T(8,128)}), f32[128,128]{0,1:T(8,128)}) %reduce-scatter.9.cloned.1.call-update) | async-done | bytes 65552 | tf_op jit(solution)/shard_map/reduce_scatter | solution.py:141
  650.7 72.3 %all-gather.6.cloned.1.call-done = bf16[8192,128]{0,1:T(8,128)(2,1)} async-done(((bf16[128,128]{0,1:T(8,128)(2,1)}), bf16[8192,128]{0,1:T(8,128)(2,1)}) %all-gather.6.cloned.1.call-update) | async-done | bytes 2097168 | tf_op jit(solution)/shard_map/all_gather | solution.py:155
  723.0 74.7 %all-gather.8.cloned.1.call-done = bf16[8192,128]{0,1:T(8,128)(2,1)} async-done(((bf16[128,128]{0,1:T(8,128)(2,1)}), bf16[8192,128]{0,1:T(8,128)(2,1)}) %all-gather.8.cloned.1.call-update) | async-done | bytes 2097168 | tf_op jit(solution)/shard_map/all_gather | solution.py:156
  818.0 131.7 %while.55 = (s32[]{:T(128)}, f32[2,128,2,64]{1,3,2,0:T(8,128)S(1)}, f32[2,128,2,64]{1,3,2,0:T(8,128)S(1)}, f32[64,128,2,64]{1,3,2,0:T(8,128)}, f32[64,128,2,64]{...) while((s32[]{:T(128)}, f32[2,128,2,64]{1,3,2,0:T(8,128)S(1)}, ...), condition=%wide.region_24.25_spmd, body=%wide.region_19.24_spmd.sunk | while | flops 482347136 | bytes 61189336 | solution.py:235
  835.9 5.7 gather_fusion.8
  901.5 5.7 gather_fusion.8
  964.2 5.3 copy.184
  971.9 129.8 %reduce-scatter.15.cloned.1.call-done = f32[128,128]{0,1:T(8,128)} async-done(((f32[8192,128]{0,1:T(8,128)}), f32[128,128]{0,1:T(8,128)}) %reduce-scatter.15.cloned.1.call-update) | async-done | bytes 65552 | tf_op jit(solution)/shard_map/reduce_scatter | solution.py:257
  1102.8 145.3 %reduce-scatter.13.cloned.1.call-done = f32[128,128]{0,1:T(8,128)} async-done(((f32[8192,128]{0,1:T(8,128)}), f32[128,128]{0,1:T(8,128)}) %reduce-scatter.13.cloned.1.call-update) | async-done | bytes 65552 | tf_op jit(solution)/shard_map/reduce_scatter | solution.py:254
  1253.0 20.9 %reduce-scatter.11.cloned.1.call-done = f32[256,128]{1,0:T(8,128)} async-done(((f32[256,512]{1,0:T(8,128)}), f32[256,128]{1,0:T(8,128)}) %reduce-scatter.11.cloned.1.call-update) | async-done | bytes 131088 | tf_op jit(solution)/shard_map/reduce_scatter | solution.py:264
  1275.5 187.6 %all-reduce.5.cloned.1.call-done = f32[4,512,128]{1,2,0:T(8,128)} async-done(((f32[4,512,128]{1,2,0:T(8,128)}), f32[4,512,128]{1,2,0:T(8,128)}) %all-reduce.5.cloned.1.call-update) | async-done | bytes 1048592 | tf_op jit(solution)/shard_map/psum | solution.py:267
  1465.7 20.8 %reduce-scatter.17.cloned.1.call-done = f32[128,128]{1,0:T(8,128)} async-done(((f32[128,512]{1,0:T(8,128)}), f32[128,128]{1,0:T(8,128)}) %reduce-scatter.17.cloned.1.call-update) | async-done | bytes 65552 | tf_op jit(solution)/shard_map/reduce_scatter | solution.py:265
  (274 shorter events, 272.4 us)
Async XLA Ops:
  7.2 39.4 %copy-start = (bf16[512,128]{1,0:T(8,128)(2,1)S(1)}, bf16[512,128]{1,0:T(8,128)(2,1)}, u32[]{:S(2)}) copy-start(bf16[512,128]{1,0:T(8,128)(2,1)} %param.18) | copy-start | bytes 393220
  19.1 15.3 %copy-start.8 = (bf16[128,512]{1,0:T(8,128)(2,1)}, bf16[128,512]{1,0:T(8,128)(2,1)S(1)}, u32[]{:S(2)}) copy-start(bf16[128,512]{1,0:T(8,128)(2,1)S(1)} %all_gather.16) | copy-start | bytes 393220
  22.2 12.2 copy-start.16
  22.2 13.1 copy-start.28
  22.2 62.9 %all-to-all-start = ((bf16[64,128,128]{1,2,0:T(8,128)(2,1)}), bf16[64,128,128]{1,2,0:T(8,128)(2,1)S(1)}, u32[]{:S(2)}, u32[]{:S(2)}) async-start(bf16[64,128,128]{1,2,0:T(8,128)(2,1)} %stack.12), calls=%async_computation | async-start | bytes 4194304 | tf_op jit(solution)/shard_map/all_to_all | solution.py:52
  34.4 84.1 %all-gather.4.cloned.1.call-start = ((), (), s32[]{:S(2)}) async-start(), calls=%async_computation.7 | async-start | bytes 2129920 | tf_op jit(solution)/shard_map/all_gather | solution.py:54
  35.3 253.2 %all-reduce.3.cloned.1.call-start = ((), (), s32[]{:S(2)}) async-start(), calls=%async_computation.8 | async-start | bytes 131072 | tf_op jit(solution)/shard_map/pmax | solution.py:94
  46.6 70.0 %copy-start.6 = (bf16[256,512]{1,0:T(8,128)(2,1)}, bf16[256,512]{1,0:T(8,128)(2,1)S(1)}, u32[]{:S(2)}) copy-start(bf16[256,512]{1,0:T(8,128)(2,1)S(1)} %all_gather.15) | copy-start | bytes 786436
  92.6 24.0 %copy-start.13 = (bf16[512,128]{1,0:T(8,128)(2,1)S(1)}, bf16[512,128]{1,0:T(8,128)(2,1)}, u32[]{:S(2)}) copy-start(bf16[512,128]{1,0:T(8,128)(2,1)} %param.19) | copy-start | bytes 393220
  116.6 385.4 %reduce-scatter.19.cloned.1.call-start = ((), (), s32[]{:S(2)}) async-start(), calls=%async_computation.17 | async-start | bytes 4259840
  361.2 287.0 %reduce-scatter.9.cloned.1.call-start = ((), (), s32[]{:S(2)}) async-start(), calls=%async_computation.9 | async-start | bytes 4259840 | tf_op jit(solution)/shard_map/reduce_scatter | solution.py:141
  371.1 279.3 %copy-start.21 = (bf16[256,128]{1,0:T(8,128)(2,1)S(1)}, bf16[256,128]{1,0:T(8,128)(2,1)}, u32[]{:S(2)}) copy-start(bf16[256,128]{1,0:T(8,128)(2,1)} %param.22) | copy-start | bytes 196612
  371.1 351.9 %all-gather.6.cloned.1.call-start = ((), (), s32[]{:S(2)}) async-start(), calls=%async_computation.10 | async-start | bytes 2129920 | tf_op jit(solution)/shard_map/all_gather | solution.py:155
  649.7 148.0 %all-gather.8.cloned.1.call-start = ((), (), s32[]{:S(2)}) async-start(), calls=%async_computation.11 | async-start | bytes 2129920 | tf_op jit(solution)/shard_map/all_gather | solution.py:156
  650.3 451.5 %reduce-scatter.15.cloned.1.call-start = ((), (), s32[]{:S(2)}) async-start(), calls=%async_computation.14 | async-start | bytes 4259840 | tf_op jit(solution)/shard_map/reduce_scatter | solution.py:257
  650.7 149.8 %copy-start.11 = (bf16[2,128,2,64]{1,0,3,2:T(2,128)(2,1)}, bf16[2,128,2,64]{1,0,3,2:T(2,128)(2,1)S(1)}, u32[]{:S(2)}) copy-start(bf16[2,128,2,64]{1,0,3,2:T(2,128)(2,1)S(1)} %copy.104) | copy-start | bytes 196612
  959.6 288.6 %reduce-scatter.13.cloned.1.call-start = ((), (), s32[]{:S(2)}) async-start(), calls=%async_computation.13 | async-start | bytes 4259840 | tf_op jit(solution)/shard_map/reduce_scatter | solution.py:254
  969.5 304.5 %reduce-scatter.11.cloned.1.call-start = ((), (), s32[]{:S(2)}) async-start(), calls=%async_computation.12 | async-start | bytes 655360 | tf_op jit(solution)/shard_map/reduce_scatter | solution.py:264
  969.6 132.2 %copy-start.9 = (bf16[128,512]{1,0:T(8,128)(2,1)S(1)}, bf16[128,512]{1,0:T(8,128)(2,1)}, u32[]{:S(2)}) copy-start(bf16[128,512]{1,0:T(8,128)(2,1)} %copy-done.8) | copy-start | bytes 393220
  971.5 491.7 %all-reduce.5.cloned.1.call-start = ((), (), s32[]{:S(2)}) async-start(), calls=%async_computation.16 | async-start | bytes 2097152 | tf_op jit(solution)/shard_map/psum | solution.py:267
  971.9 278.4 %copy-start.15 = (bf16[512,128]{1,0:T(8,128)(2,1)S(1)}, bf16[512,128]{1,0:T(8,128)(2,1)}, u32[]{:S(2)}) copy-start(bf16[512,128]{1,0:T(8,128)(2,1)} %param.20) | copy-start | bytes 393220
  1102.8 147.8 %copy-start.17 = (bf16[512,128]{1,0:T(8,128)(2,1)S(1)}, bf16[512,128]{1,0:T(8,128)(2,1)}, u32[]{:S(2)}) copy-start(bf16[512,128]{1,0:T(8,128)(2,1)} %param.21) | copy-start | bytes 393220
  1102.8 147.8 %copy-start.22 = (f32[128,128]{0,1:T(8,128)S(1)}, f32[128,128]{0,1:T(8,128)}, u32[]{:S(2)}) copy-start(f32[128,128]{0,1:T(8,128)} %reduce-scatter.15.cloned.1.call-done) | copy-start | bytes 196612
  1250.3 236.2 %reduce-scatter.17.cloned.1.call-start = ((), (), s32[]{:S(2)}) async-start(), calls=%async_computation.15 | async-start | bytes 327680 | tf_op jit(solution)/shard_map/reduce_scatter | solution.py:265
  (30 other events, 60.7 us)
Sparse Core Ops, SparseCore 0:
  38.6 79.8 all-gather.3
  122.5 165.9 all-reduce.2
  361.3 140.6 reduce-scatter.18
  506.0 142.1 reduce-scatter.8
  651.5 71.4 all-gather.5
  726.3 71.3 all-gather.7
  959.7 142.0 reduce-scatter.14
  1105.9 142.1 reduce-scatter.12
  1250.8 23.1 reduce-scatter.10
  1278.2 184.9 all-reduce.4
  1465.7 20.7 reduce-scatter.16
